TPU v7x, 512 devices: a whole 4x4x16 slice. The times are simulated.
512 devices in a mesh: seq: 64 (over y, z_lo, core), head: 8 (over z_hi, x).
Axes of the slice: x: 4, y: 4, z: 16 (z_hi: 2, z_lo: 8; z = z_hi * 8 + z_lo), core: 2. Of those that a mesh axis runs over, the one named last changes fastest.
Arguments:
- queries: bfloat16 [16384, 32, 128], P('seq', 'head'), may hold values from -48 to 48
- keys: bfloat16 [16384, 32, 128], P('seq', 'head'), may hold values from -6 to 6
- values: bfloat16 [16384, 32, 128], P('seq', 'head'), may hold values from -6 to 6
- attended: bfloat16 [16384, 32, 128], P('seq', 'head'), may hold values from -6 to 6
- out_grads: bfloat16 [16384, 32, 128], P('seq', 'head'), may hold values from -6 to 6
Outputs:
- grad_queries: bfloat16 [16384, 32, 128], P(('seq', 'head'))
- grad_keys: bfloat16 [16384, 32, 128], P(('seq', 'head'))
- grad_values: bfloat16 [16384, 32, 128], P(('seq', 'head'))
All inputs are finite; a program needn't handle non-finite values.
Results may differ from a plain program's by a relative error of at most 0.005.
Values may be sent and summed in bfloat16 or wider, within the bound.
A program may use at most 64 MiB of HBM per device.

v0:
```python
import jax
import jax.numpy as jnp
from jax import lax
from jax.sharding import PartitionSpec as P

SPAN = 4


def from_behind(block, axis, distance):
    devices = range(lax.axis_size(axis))
    route = [(i - distance, i) for i in devices if i - distance in devices]
    return lax.ppermute(block, axis, route)


def block_scores(query_rows, key_rows, scaling, diagonal):
    scores = (
        jnp.einsum("qhd,khd->hqk", query_rows, key_rows, preferred_element_type=jnp.float32)
        * scaling
    )
    if diagonal:
        row_count = scores.shape[1]
        allowed = jnp.arange(row_count)[None, :] <= jnp.arange(row_count)[:, None]
        scores = jnp.where(allowed[None, :, :], scores, -jnp.inf)
    return scores


def pair_grads(
    query_rows, grad_rows, log_total, correction, key_rows, value_rows, scaling, diagonal
):
    scores = block_scores(query_rows, key_rows, scaling, diagonal)
    weights = jnp.exp(scores - log_total[:, :, None])
    weights_low = weights.astype(jnp.bfloat16)
    grad_value = jnp.einsum(
        "hqk,qhd->khd", weights_low, grad_rows, preferred_element_type=jnp.float32
    )
    grad_weights = jnp.einsum(
        "qhd,khd->hqk", grad_rows, value_rows, preferred_element_type=jnp.float32
    )
    grad_scores = (weights * (grad_weights - correction[:, :, None]) * scaling).astype(jnp.bfloat16)
    grad_query = jnp.einsum(
        "hqk,khd->qhd", grad_scores, key_rows, preferred_element_type=jnp.float32
    )
    grad_key = jnp.einsum(
        "hqk,qhd->khd", grad_scores, query_rows, preferred_element_type=jnp.float32
    )
    return (grad_query, grad_key, grad_value)


def body(queries, keys, values, attended, out_grads):
    local_query, local_key, local_value, local_output, local_grad = (
        queries,
        keys,
        values,
        attended,
        out_grads,
    )
    row_count = local_query.shape[0]
    head_count = local_query.shape[1]
    scaling = local_query.shape[2] ** (-0.5)
    position = lax.axis_index("seq") % SPAN
    earlier = [from_behind((local_key, local_value), "seq", offset) for offset in range(1, SPAN)]
    blocks = [(local_key, local_value)] + earlier

    def live_scores(key_rows):
        return block_scores(local_query, key_rows, scaling, False)

    def dead_scores(key_rows):
        return jnp.full((head_count, row_count, row_count), -jnp.inf, jnp.float32)

    running_max = jnp.full((head_count, row_count), -jnp.inf, jnp.float32)
    running_sum = jnp.zeros((head_count, row_count), jnp.float32)
    for offset in range(SPAN):
        if offset == 0:
            scores = block_scores(local_query, blocks[0][0], scaling, True)
        else:
            scores = lax.cond(position >= offset, live_scores, dead_scores, blocks[offset][0])
        new_max = jnp.maximum(running_max, jnp.max(scores, axis=2))
        running_sum = running_sum * jnp.exp(running_max - new_max) + jnp.sum(
            jnp.exp(scores - new_max[:, :, None]), axis=2
        )
        running_max = new_max
    log_total = running_max + jnp.log(running_sum)
    correction = jnp.einsum(
        "qhd,qhd->hq", local_grad, local_output, preferred_element_type=jnp.float32
    )
    grad_query, grad_key, grad_value = pair_grads(
        local_query, local_grad, log_total, correction, local_key, local_value, scaling, True
    )

    def remote_pair(key_rows, value_rows):
        return pair_grads(
            local_query, local_grad, log_total, correction, key_rows, value_rows, scaling, False
        )

    def skip_pair(key_rows, value_rows):
        empty = jnp.zeros(local_query.shape, jnp.float32)
        return (empty, empty, empty)

    last_offset = SPAN
    for offset in range(1, last_offset):
        key_rows, value_rows = blocks[offset]
        piece_query, piece_key, piece_value = lax.cond(
            position >= offset, remote_pair, skip_pair, key_rows, value_rows
        )
        grad_query = grad_query + piece_query
        back_key, back_value = from_behind((piece_key, piece_value), "seq", -offset)
        grad_key = grad_key + back_key
        grad_value = grad_value + back_value
    return (
        lax.all_to_all(
            grad_query.astype(jnp.bfloat16), "head", split_axis=0, concat_axis=1, tiled=True
        ),
        lax.all_to_all(
            grad_key.astype(jnp.bfloat16), "head", split_axis=0, concat_axis=1, tiled=True
        ),
        lax.all_to_all(
            grad_value.astype(jnp.bfloat16), "head", split_axis=0, concat_axis=1, tiled=True
        ),
    )


def solution(mesh):
    placed = (
        P("seq", "head", None),
        P("seq", "head", None),
        P("seq", "head", None),
        P("seq", "head", None),
        P("seq", "head", None),
    )
    return jax.shard_map(
        body,
        mesh=mesh,
        in_specs=placed,
        out_specs=(
            P(("seq", "head"), None, None),
            P(("seq", "head"), None, None),
            P(("seq", "head"), None, None),
        ),
        check_vma=False,
    )
```

profile of v0, /device:TPU:56, one launch (start us, length us, event | category | flops | bytes accessed | tf_op | source)
XLA Modules:
  0.0 221.4 jit_solution(4676278899118936926)
XLA Ops:
  2.4 3.9 %collective-permute-start.1 = (bf16[256,4,128]{2,0,1:T(8,128)(2,1)}, bf16[256,4,128]{2,0,1:T(8,128)(2,1)S(1)}, u32[]{:S(2)}, u32[]{:S(2)}) collective-permute-start(bf16[256,4,128]{2,0,1:T(8,128)(2,1)} %copy.48), channel_id=1, source_target_pairs={{0,16},{8,24},{16,32},{24,40},{32,48},{40,56},{48,64},{56,72},{64,... | collective-permute-start | bytes 786440 | tf_op jit(solution)/shard_map/ppermute | solution.py:12
  6.3 1.9 collective-permute-start
  8.3 6.7 %collective-permute-start.2 = (bf16[256,4,128]{2,0,1:T(8,128)(2,1)}, bf16[256,4,128]{2,0,1:T(8,128)(2,1)S(1)}, u32[]{:S(2)}, u32[]{:S(2)}) collective-permute-start(bf16[256,4,128]{2,0,1:T(8,128)(2,1)} %copy.48), channel_id=1, source_target_pairs={{0,24},{8,32},{16,40},{24,48},{32,56},{40,64},{48,72},{56,80},{64,... | collective-permute-start | bytes 786440 | tf_op jit(solution)/shard_map/ppermute | solution.py:12
  15.7 3.8 %collective-permute-start.4 = (bf16[256,4,128]{2,0,1:T(8,128)(2,1)}, bf16[256,4,128]{2,0,1:T(8,128)(2,1)}, u32[]{:S(2)}, u32[]{:S(2)}) collective-permute-start(bf16[256,4,128]{2,0,1:T(8,128)(2,1)} %copy.56), channel_id=1, source_target_pairs={{0,16},{8,24},{16,32},{24,40},{32,48},{40,56},{48,64},{56,72},{64,... | collective-permute-start | bytes 786440 | tf_op jit(solution)/shard_map/ppermute | solution.py:12
  19.5 1.9 collective-permute-start.3
  23.2 8.3 %collective-permute-done.2 = bf16[256,4,128]{2,0,1:T(8,128)(2,1)S(1)} collective-permute-done((bf16[256,4,128]{2,0,1:T(8,128)(2,1)}, bf16[256,4,128]{2,0,1:T(8,128)(2,1)S(1)}, u32[]{:S(2)}, u32[]{:S(2)}) %collective-permute-start.2) | collective-permute-done | bytes 262176 | tf_op jit(solution)/shard_map/ppermute | solution.py:12
  31.5 1.9 collective-permute-start.5
  36.7 2.5 %conditional.7 = (f32[4,256,256]{1,2,0:T(8,128)}, f32[4,256]{1,0:T(4,128)}, f32[4,256,1]{1,0,2:T(4,128)S(1)}) conditional(s32[]{:T(128)} %convert_element_type.46, () %tuple.64, (bf16[256,4,128]{2,1,0:T(4,128)(2,1)S(1)}, bf16[256,4,128]{2,0,1:T(8,128)(2,1)S(1)}) %tuple.108), branch_computations={%region_4.5_spmd, %region_5.7_spmd} | conditional | flops 67632128 | bytes 1585176 | solution.py:76
  43.4 2.6 %conditional.9 = (f32[256,4,128]{2,0,1:T(8,128)S(1)}, f32[256,4,128]{2,0,1:T(8,128)S(1)}, f32[256,4,128]{2,0,1:T(8,128)S(1)}) conditional(s32[]{:T(128)} %convert_element_type.45, () %tuple.68, (bf16[256,4,128]{2,1,0:T(4,128)(2,1)S(1)}, bf16[256,4,128]{2,0,1:T(8,128)(2,1)S(1)}, f32[4,256]{1,0:T(4,128)S(1)}, bf16[256,4,128]{2,1,0:T(4,128)(2,1)S(1)}, ...), branch_computations={%region_14.15_spmd, %region_15.16_spmd} | conditional | flops 337379328 | bytes 8134680 | solution.py:102
  47.2 2.6 %conditional.10 = (f32[256,4,128]{2,0,1:T(8,128)S(1)}, f32[256,4,128]{2,0,1:T(8,128)S(1)}, f32[256,4,128]{2,0,1:T(8,128)S(1)}) conditional(s32[]{:T(128)} %convert_element_type.46, () %tuple.70, (bf16[256,4,128]{2,1,0:T(4,128)(2,1)S(1)}, bf16[256,4,128]{2,0,1:T(8,128)(2,1)S(1)}, f32[4,256]{1,0:T(4,128)S(1)}, bf16[256,4,128]{2,1,0:T(4,128)(2,1)S(1)}, ...), branch_computations={%region_16.17_spmd, %region_17.18_spmd} | conditional | flops 337379328 | bytes 8134680 | solution.py:102
  53.7 15.2 %all-to-all-start = ((bf16[256,4,128]{2,1,0:T(4,128)(2,1)}), bf16[256,4,128]{2,1,0:T(4,128)(2,1)S(1)}, u32[]{:S(2)}, u32[]{:S(2)}) async-start(bf16[256,4,128]{2,1,0:T(4,128)(2,1)} %copy.69), calls=%async_computation | async-start | bytes 524288 | tf_op jit(solution)/shard_map/all_to_all | solution.py:110
  68.9 1.9 collective-permute-start.6
  70.8 14.6 %collective-permute-start.7 = (f32[256,4,128]{2,0,1:T(8,128)S(1)}, f32[256,4,128]{2,0,1:T(8,128)S(1)}, u32[]{:S(2)}, u32[]{:S(2)}) collective-permute-start(f32[256,4,128]{2,0,1:T(8,128)S(1)} %copy-done.17), channel_id=1, source_target_pairs={{16,0},{24,8},{32,16},{40,24},{48,32},{56,40},{64,48},{72,56},{80,... | collective-permute-start | bytes 1572872 | tf_op jit(solution)/shard_map/ppermute | solution.py:12
  85.5 10.2 %collective-permute-start.8 = (f32[256,4,128]{2,0,1:T(8,128)}, f32[256,4,128]{2,0,1:T(8,128)S(1)}, u32[]{:S(2)}, u32[]{:S(2)}) collective-permute-start(f32[256,4,128]{2,0,1:T(8,128)} %copy-done.19), channel_id=1, source_target_pairs={{24,0},{32,8},{40,16},{48,24},{56,32},{64,40},{72,48},{80,56},{88,... | collective-permute-start | bytes 1572872 | tf_op jit(solution)/shard_map/ppermute | solution.py:12
  96.0 13.0 %collective-permute-done.7 = f32[256,4,128]{2,0,1:T(8,128)S(1)} collective-permute-done((f32[256,4,128]{2,0,1:T(8,128)S(1)}, f32[256,4,128]{2,0,1:T(8,128)S(1)}, u32[]{:S(2)}, u32[]{:S(2)}) %collective-permute-start.7) | collective-permute-done | bytes 524320 | tf_op jit(solution)/shard_map/ppermute | solution.py:12
  109.0 9.6 %collective-permute-done.8 = f32[256,4,128]{2,0,1:T(8,128)S(1)} collective-permute-done((f32[256,4,128]{2,0,1:T(8,128)}, f32[256,4,128]{2,0,1:T(8,128)S(1)}, u32[]{:S(2)}, u32[]{:S(2)}) %collective-permute-start.8) | collective-permute-done | bytes 524320 | tf_op jit(solution)/shard_map/ppermute | solution.py:12
  119.6 14.2 %all-to-all-start.1 = ((bf16[256,4,128]{2,1,0:T(4,128)(2,1)}), bf16[256,4,128]{2,1,0:T(4,128)(2,1)S(1)}, u32[]{:S(2)}, u32[]{:S(2)}) async-start(bf16[256,4,128]{2,1,0:T(4,128)(2,1)} %copy.72), calls=%async_computation.1 | async-start | bytes 524288 | tf_op jit(solution)/shard_map/all_to_all | solution.py:113
  133.8 1.9 collective-permute-start.9
  135.8 11.5 %collective-permute-start.10 = (f32[256,4,128]{2,0,1:T(8,128)S(1)}, f32[256,4,128]{2,0,1:T(8,128)S(1)}, u32[]{:S(2)}, u32[]{:S(2)}) collective-permute-start(f32[256,4,128]{2,0,1:T(8,128)S(1)} %copy-done.15), channel_id=1, source_target_pairs={{16,0},{24,8},{32,16},{40,24},{48,32},{56,40},{64,48},{72,56},{80,... | collective-permute-start | bytes 1572872 | tf_op jit(solution)/shard_map/ppermute | solution.py:12
  147.3 1.9 collective-permute-start.11
  149.5 10.8 %collective-permute-done.10 = f32[256,4,128]{2,0,1:T(8,128)S(1)} collective-permute-done((f32[256,4,128]{2,0,1:T(8,128)S(1)}, f32[256,4,128]{2,0,1:T(8,128)S(1)}, u32[]{:S(2)}, u32[]{:S(2)}) %collective-permute-start.10) | collective-permute-done | bytes 524320 | tf_op jit(solution)/shard_map/ppermute | solution.py:12
  160.3 19.4 %collective-permute-done.11 = f32[256,4,128]{2,0,1:T(8,128)S(1)} collective-permute-done((f32[256,4,128]{2,0,1:T(8,128)}, f32[256,4,128]{2,0,1:T(8,128)S(1)}, u32[]{:S(2)}, u32[]{:S(2)}) %collective-permute-start.11) | collective-permute-done | bytes 524320 | tf_op jit(solution)/shard_map/ppermute | solution.py:12
  180.7 24.0 %all-to-all-start.2 = ((bf16[256,4,128]{2,1,0:T(4,128)(2,1)}), bf16[256,4,128]{2,1,0:T(4,128)(2,1)S(1)}, u32[]{:S(2)}, u32[]{:S(2)}) async-start(bf16[256,4,128]{2,1,0:T(4,128)(2,1)} %copy.75), calls=%async_computation.2 | async-start | bytes 524288 | tf_op jit(solution)/shard_map/all_to_all | solution.py:116
  206.2 14.4 %all-to-all-done.2 = bf16[256,4,128]{2,1,0:T(4,128)(2,1)S(1)} async-done(((bf16[256,4,128]{2,1,0:T(4,128)(2,1)}), bf16[256,4,128]{2,1,0:T(4,128)(2,1)S(1)}, u32[]{:S(2)}, u32[]{:S(2)}) %all-to-all-start.2) | async-done | bytes 262176 | tf_op jit(solution)/shard_map/all_to_all | solution.py:116
  (99 shorter events, 31.5 us)
Async XLA Ops:
  0.6 14.3 %copy-start.8 = (bf16[256,4,128]{2,1,0:T(4,128)(2,1)S(1)}, bf16[256,4,128]{2,1,0:T(4,128)(2,1)}, u32[]{:S(2)}) copy-start(bf16[256,4,128]{2,1,0:T(4,128)(2,1)} %param.19) | copy-start | bytes 786436
  2.4 19.1 %copy-start = (bf16[256,4,128]{2,1,0:T(4,128)(2,1)S(1)}, bf16[256,4,128]{2,1,0:T(4,128)(2,1)}, u32[]{:S(2)}) copy-start(bf16[256,4,128]{2,1,0:T(4,128)(2,1)} %param.17) | copy-start | bytes 786436
  2.4 19.1 %copy-start.6 = (bf16[256,4,128]{2,1,0:T(4,128)(2,1)S(1)}, bf16[256,4,128]{2,1,0:T(4,128)(2,1)}, u32[]{:S(2)}) copy-start(bf16[256,4,128]{2,1,0:T(4,128)(2,1)} %param.18) | copy-start | bytes 786436
  2.4 33.4 %collective-permute-start.1 = (bf16[256,4,128]{2,0,1:T(8,128)(2,1)}, bf16[256,4,128]{2,0,1:T(8,128)(2,1)S(1)}, u32[]{:S(2)}, u32[]{:S(2)}) collective-permute-start(bf16[256,4,128]{2,0,1:T(8,128)(2,1)} %copy.48), channel_id=1, source_target_pairs={{0,16},{8,24},{16,32},{24,40},{32,48},{40,56},{48,64},{56,72},{64,... | collective-permute-start | bytes 786440 | tf_op jit(solution)/shard_map/ppermute | solution.py:12
  6.3 27.8 %collective-permute-start = (bf16[256,4,128]{2,0,1:T(8,128)(2,1)}, bf16[256,4,128]{2,0,1:T(8,128)(2,1)S(1)}, u32[]{:S(2)}, u32[]{:S(2)}) collective-permute-start(bf16[256,4,128]{2,0,1:T(8,128)(2,1)} %copy.48), channel_id=1, source_target_pairs={{0,8},{8,16},{16,24},{24,32},{32,40},{40,48},{48,56},{56,64},{64,7... | collective-permute-start | bytes 786440 | tf_op jit(solution)/shard_map/ppermute | solution.py:12
  8.3 23.2 %collective-permute-start.2 = (bf16[256,4,128]{2,0,1:T(8,128)(2,1)}, bf16[256,4,128]{2,0,1:T(8,128)(2,1)S(1)}, u32[]{:S(2)}, u32[]{:S(2)}) collective-permute-start(bf16[256,4,128]{2,0,1:T(8,128)(2,1)} %copy.48), channel_id=1, source_target_pairs={{0,24},{8,32},{16,40},{24,48},{32,56},{40,64},{48,72},{56,80},{64,... | collective-permute-start | bytes 786440 | tf_op jit(solution)/shard_map/ppermute | solution.py:12
  15.7 30.4 %collective-permute-start.4 = (bf16[256,4,128]{2,0,1:T(8,128)(2,1)}, bf16[256,4,128]{2,0,1:T(8,128)(2,1)}, u32[]{:S(2)}, u32[]{:S(2)}) collective-permute-start(bf16[256,4,128]{2,0,1:T(8,128)(2,1)} %copy.56), channel_id=1, source_target_pairs={{0,16},{8,24},{16,32},{24,40},{32,48},{40,56},{48,64},{56,72},{64,... | collective-permute-start | bytes 786440 | tf_op jit(solution)/shard_map/ppermute | solution.py:12
  19.5 23.9 %collective-permute-start.3 = (bf16[256,4,128]{2,0,1:T(8,128)(2,1)}, bf16[256,4,128]{2,0,1:T(8,128)(2,1)}, u32[]{:S(2)}, u32[]{:S(2)}) collective-permute-start(bf16[256,4,128]{2,0,1:T(8,128)(2,1)} %copy.56), channel_id=1, source_target_pairs={{0,8},{8,16},{16,24},{24,32},{32,40},{40,48},{48,56},{56,64},{64,7... | collective-permute-start | bytes 786440 | tf_op jit(solution)/shard_map/ppermute | solution.py:12
  31.5 19.1 %collective-permute-start.5 = (bf16[256,4,128]{2,0,1:T(8,128)(2,1)}, bf16[256,4,128]{2,0,1:T(8,128)(2,1)}, u32[]{:S(2)}, u32[]{:S(2)}) collective-permute-start(bf16[256,4,128]{2,0,1:T(8,128)(2,1)} %copy.56), channel_id=1, source_target_pairs={{0,24},{8,32},{16,40},{24,48},{32,56},{40,64},{48,72},{56,80},{64,... | collective-permute-start | bytes 786440 | tf_op jit(solution)/shard_map/ppermute | solution.py:12
  46.1 3.7 %copy-start.7 = (bf16[256,4,128]{2,1,0:T(4,128)(2,1)S(1)}, bf16[256,4,128]{2,1,0:T(4,128)(2,1)}, u32[]{:S(2)}) copy-start(bf16[256,4,128]{2,1,0:T(4,128)(2,1)} %param.18) | copy-start | bytes 786436
  51.1 1.7 copy-start.18
  52.8 16.1 %copy-start.13 = (f32[256,4,128]{2,0,1:T(8,128)S(1)}, f32[256,4,128]{2,0,1:T(8,128)}, u32[]{:S(2)}) copy-start(f32[256,4,128]{2,0,1:T(8,128)} %copy-done.12) | copy-start | bytes 1572868
  53.7 17.1 %copy-start.17 = (f32[256,4,128]{2,0,1:T(8,128)S(1)}, f32[256,4,128]{2,0,1:T(8,128)}, u32[]{:S(2)}) copy-start(f32[256,4,128]{2,0,1:T(8,128)} %copy-done.16) | copy-start | bytes 1572868
  53.7 65.9 %all-to-all-start = ((bf16[256,4,128]{2,1,0:T(4,128)(2,1)}), bf16[256,4,128]{2,1,0:T(4,128)(2,1)S(1)}, u32[]{:S(2)}, u32[]{:S(2)}) async-start(bf16[256,4,128]{2,1,0:T(4,128)(2,1)} %copy.69), calls=%async_computation | async-start | bytes 524288 | tf_op jit(solution)/shard_map/all_to_all | solution.py:110
  68.9 27.1 %collective-permute-start.6 = (f32[256,4,128]{2,0,1:T(8,128)S(1)}, f32[256,4,128]{2,0,1:T(8,128)S(1)}, u32[]{:S(2)}, u32[]{:S(2)}) collective-permute-start(f32[256,4,128]{2,0,1:T(8,128)S(1)} %copy-done.13), channel_id=1, source_target_pairs={{8,0},{16,8},{24,16},{32,24},{40,32},{48,40},{56,48},{64,56},{72,6... | collective-permute-start | bytes 1572872 | tf_op jit(solution)/shard_map/ppermute | solution.py:12
  70.8 38.1 %collective-permute-start.7 = (f32[256,4,128]{2,0,1:T(8,128)S(1)}, f32[256,4,128]{2,0,1:T(8,128)S(1)}, u32[]{:S(2)}, u32[]{:S(2)}) collective-permute-start(f32[256,4,128]{2,0,1:T(8,128)S(1)} %copy-done.17), channel_id=1, source_target_pairs={{16,0},{24,8},{32,16},{40,24},{48,32},{56,40},{64,48},{72,56},{80,... | collective-permute-start | bytes 1572872 | tf_op jit(solution)/shard_map/ppermute | solution.py:12
  85.5 33.1 %collective-permute-start.8 = (f32[256,4,128]{2,0,1:T(8,128)}, f32[256,4,128]{2,0,1:T(8,128)S(1)}, u32[]{:S(2)}, u32[]{:S(2)}) collective-permute-start(f32[256,4,128]{2,0,1:T(8,128)} %copy-done.19), channel_id=1, source_target_pairs={{24,0},{32,8},{40,16},{48,24},{56,32},{64,40},{72,48},{80,56},{88,... | collective-permute-start | bytes 1572872 | tf_op jit(solution)/shard_map/ppermute | solution.py:12
  118.7 15.2 %copy-start.11 = (f32[256,4,128]{2,0,1:T(8,128)S(1)}, f32[256,4,128]{2,0,1:T(8,128)}, u32[]{:S(2)}) copy-start(f32[256,4,128]{2,0,1:T(8,128)} %copy-done.10) | copy-start | bytes 1572868
  118.7 17.1 %copy-start.15 = (f32[256,4,128]{2,0,1:T(8,128)S(1)}, f32[256,4,128]{2,0,1:T(8,128)}, u32[]{:S(2)}) copy-start(f32[256,4,128]{2,0,1:T(8,128)} %copy-done.14) | copy-start | bytes 1572868
  119.6 61.1 %all-to-all-start.1 = ((bf16[256,4,128]{2,1,0:T(4,128)(2,1)}), bf16[256,4,128]{2,1,0:T(4,128)(2,1)S(1)}, u32[]{:S(2)}, u32[]{:S(2)}) async-start(bf16[256,4,128]{2,1,0:T(4,128)(2,1)} %copy.72), calls=%async_computation.1 | async-start | bytes 524288 | tf_op jit(solution)/shard_map/all_to_all | solution.py:113
  133.8 15.7 %collective-permute-start.9 = (f32[256,4,128]{2,0,1:T(8,128)S(1)}, f32[256,4,128]{2,0,1:T(8,128)S(1)}, u32[]{:S(2)}, u32[]{:S(2)}) collective-permute-start(f32[256,4,128]{2,0,1:T(8,128)S(1)} %copy-done.11), channel_id=1, source_target_pairs={{8,0},{16,8},{24,16},{32,24},{40,32},{48,40},{56,48},{64,56},{72,6... | collective-permute-start | bytes 1572872 | tf_op jit(solution)/shard_map/ppermute | solution.py:12
  135.8 24.5 %collective-permute-start.10 = (f32[256,4,128]{2,0,1:T(8,128)S(1)}, f32[256,4,128]{2,0,1:T(8,128)S(1)}, u32[]{:S(2)}, u32[]{:S(2)}) collective-permute-start(f32[256,4,128]{2,0,1:T(8,128)S(1)} %copy-done.15), channel_id=1, source_target_pairs={{16,0},{24,8},{32,16},{40,24},{48,32},{56,40},{64,48},{72,56},{80,... | collective-permute-start | bytes 1572872 | tf_op jit(solution)/shard_map/ppermute | solution.py:12
  147.3 32.4 %collective-permute-start.11 = (f32[256,4,128]{2,0,1:T(8,128)}, f32[256,4,128]{2,0,1:T(8,128)S(1)}, u32[]{:S(2)}, u32[]{:S(2)}) collective-permute-start(f32[256,4,128]{2,0,1:T(8,128)} %copy-done.18), channel_id=1, source_target_pairs={{24,0},{32,8},{40,16},{48,24},{56,32},{64,40},{72,48},{80,56},{88,... | collective-permute-start | bytes 1572872 | tf_op jit(solution)/shard_map/ppermute | solution.py:12
  180.7 39.9 %all-to-all-start.2 = ((bf16[256,4,128]{2,1,0:T(4,128)(2,1)}), bf16[256,4,128]{2,1,0:T(4,128)(2,1)S(1)}, u32[]{:S(2)}, u32[]{:S(2)}) async-start(bf16[256,4,128]{2,1,0:T(4,128)(2,1)} %copy.75), calls=%async_computation.2 | async-start | bytes 524288 | tf_op jit(solution)/shard_map/all_to_all | solution.py:116
  (12 other events, 13.2 us)
where the time goes:
time: 222 us; the launch traced here: 221 us
  starting transfers between devices  116 us (52%)
  waiting for transfers between devices  75.4 us (34%)
  local copies, waits for them, and re-layouts  14 us (6%)
  matrix products  9.49 us (4%)
  other arithmetic  5.63 us (3%)
    ppermute x12, starting transfers between devices, from_behind(): return lax.ppermute(block, axis, route)  62.2 us
    ppermute x12, waiting for transfers between devices, from_behind(): return lax.ppermute(block, axis, route)  61.1 us
    all_to_all x1, starting transfers between devices, body(): lax.all_to_all(grad_value.astype(jnp.bfloat16), 'head', split_axis=0, con...  24 us
    all_to_all x1, starting transfers between devices, body(): lax.all_to_all(grad_query.astype(jnp.bfloat16), 'head', split_axis=0, con...  15.2 us
    all_to_all x1, waiting for transfers between devices, body(): lax.all_to_all(grad_value.astype(jnp.bfloat16), 'head', split_axis=0, con...  14.4 us
    all_to_all x1, starting transfers between devices, body(): lax.all_to_all(grad_key.astype(jnp.bfloat16), 'head', split_axis=0, conca...  14.2 us
    unnamed x44, local copies, waits for them, and re-layouts  6.63 us
  transfers between devices with their start and end apart: 15, of which 6 were waited for; matrix products, arithmetic and copies ran while one was open for 9% of the time, Pallas kernels for 0%

commit v1 on v0

v1 whole, which is shorter than its diff:
```python
import functools

import jax
import jax.numpy as jnp
from jax import lax
from jax.experimental import pallas as pl
from jax.experimental.pallas import tpu as pltpu
from jax.sharding import PartitionSpec as P

MESH = pl.DeviceIdType.MESH
BF16 = jnp.bfloat16
F32 = jnp.float32
SPAN = 4
TOK = 256
HL = 4
HD = 128
LEN = SPAN * TOK
HEADS = 32
PEERS = 32
ROWS = 32
SCALE = HD**-0.5

NT = (((1,), (1,)), ((), ()))


def dot(a, b):
    return jnp.dot(a, b, preferred_element_type=F32)


def dot_nt(a, b):
    return lax.dot_general(a, b, NT, preferred_element_type=F32)


def kernel(
    q_ref, k_ref, v_ref, o_ref, g_ref,
    dq_out, dk_out, dv_out,
    wide, send_in, send_corr, local_o, full, corr, grads, landed,
    in_send, in_recv, c_send, c_recv, out_send, out_recv, own_sem,
):
    seq = lax.axis_index("seq")
    head = lax.axis_index("head")
    base = (seq // SPAN) * SPAN
    place = seq % SPAN
    zh, x = head // 4, head % 4

    def peer(m):
        d_head, d_place = m // SPAN, m % SPAN
        to_zh = (zh + d_head // 4) % 2
        to_x = (x + d_head % 4) % 4
        to_place = (place + d_place) % SPAN
        return to_zh * 4 + to_x, to_place

    def source(m):
        d_head, d_place = m // SPAN, m % SPAN
        from_zh = (zh + d_head // 4) % 2
        from_x = (x + 4 - d_head % 4) % 4
        from_place = (place + SPAN - d_place) % SPAN
        return from_zh * 4 + from_x, from_place

    barrier = pltpu.get_barrier_semaphore()

    def greet(m, carry):
        to_head, to_place = source(m)
        pl.semaphore_signal(
            barrier, inc=1, device_id=(base + to_place, to_head), device_id_type=MESH
        )
        return carry

    lax.fori_loop(1, PEERS, greet, 0)

    def split_heads(ref, store):
        wide[...] = ref[...].astype(F32)
        for h in range(HL):
            store(h, wide[pl.ds(h, TOK, HL), :].astype(BF16))

    def store_in(a):
        def store(h, rows):
            send_in[a, h] = rows

        return store

    def store_o(h, rows):
        local_o[h] = rows

    def in_copy(a, d):
        to_place = (place + d) % SPAN
        return pltpu.make_async_remote_copy(
            src_ref=send_in.at[a, to_place],
            dst_ref=full.at[a, place],
            send_sem=in_send.at[a, d],
            recv_sem=in_recv.at[a, d],
            device_id=(base + to_place, head),
            device_id_type=MESH,
        )

    def corr_copy(d):
        to_place = (place + d) % SPAN
        return pltpu.make_async_remote_copy(
            src_ref=send_corr.at[to_place],
            dst_ref=corr.at[place],
            send_sem=c_send.at[d],
            recv_sem=c_recv.at[d],
            device_id=(base + to_place, head),
            device_id_type=MESH,
        )

    refs = (k_ref, q_ref, g_ref, v_ref)
    order = (2, 1, 3)
    split_heads(refs[0], store_in(0))
    pl.semaphore_wait(barrier, PEERS - 1)
    for a in range(4):
        if a:
            split_heads(refs[a], store_in(a))
        for d in order:
            in_copy(a, d).start()
    split_heads(o_ref, store_o)
    ones = jnp.ones((8, HD), BF16)
    for h in range(HL):
        prod = send_in[2, h].astype(F32) * local_o[h].astype(F32)
        high = prod.astype(BF16)
        low = (prod - high.astype(F32)).astype(BF16)
        send_corr[h] = dot_nt(ones, high) + dot_nt(ones, low)
    for d in order:
        corr_copy(d).start()
    for a in range(4):
        full[a, place] = send_in[a, place]
    corr[place] = send_corr[place]
    for a in range(4):
        for d in order:
            in_copy(a, d).wait()
    for d in order:
        corr_copy(d).wait()

    keys_t = full[0].reshape(LEN, HD).T
    row = lax.broadcasted_iota(jnp.int32, (TOK, TOK), 0)
    col = lax.broadcasted_iota(jnp.int32, (TOK, TOK), 1)
    dk_acc = [jnp.zeros((TOK, HD), F32) for _ in range(SPAN)]
    dv_acc = [jnp.zeros((TOK, HD), F32) for _ in range(SPAN)]
    for i in range(SPAN):
        q = full[1, i]
        g = full[2, i]
        c = corr[i][0:1, :]
        scores = []
        for j in range(i + 1):
            s = dot_nt(full[0, j], q) * SCALE
            if i == j:
                s = jnp.where(row <= col, s, -jnp.inf)
            scores.append(s)
        top = jnp.max(scores[0], axis=0, keepdims=True)
        for s in scores[1:]:
            top = jnp.maximum(top, jnp.max(s, axis=0, keepdims=True))
        exps = [jnp.exp(s - top) for s in scores]
        total = jnp.sum(exps[0], axis=0, keepdims=True)
        for e in exps[1:]:
            total = total + jnp.sum(e, axis=0, keepdims=True)
        inv = 1.0 / total
        dq_t = jnp.zeros((HD, TOK), F32)
        for j in range(i + 1):
            w = exps[j] * inv
            dv_acc[j] = dv_acc[j] + dot(w.astype(BF16), g)
            gw = dot_nt(full[3, j], g)
            ds = (w * (gw - c)).astype(BF16)
            dk_acc[j] = dk_acc[j] + dot(ds, q)
            dq_t = dq_t + dot(keys_t[:, j * TOK : (j + 1) * TOK], ds)
        grads[0, i] = (dq_t * SCALE).T.astype(BF16)
    for j in range(SPAN):
        grads[1, j] = (dk_acc[j] * SCALE).astype(BF16)
        grads[2, j] = dv_acc[j].astype(BF16)

    mine = head * HL + place

    def out_copy(m):
        to_head, to_place = peer(m)
        return pltpu.make_async_remote_copy(
            src_ref=grads.at[:, to_place, pl.ds(pl.multiple_of(to_head * ROWS, ROWS), ROWS)],
            dst_ref=landed.at[:, mine],
            send_sem=out_send.at[m],
            recv_sem=out_recv.at[m],
            device_id=(base + to_place, to_head),
            device_id_type=MESH,
        )

    def send(t, carry):
        out_copy(PEERS - 1 - t).start()
        return carry

    def wait(t, carry):
        out_copy(PEERS - 1 - t).wait()
        return carry

    lax.fori_loop(0, PEERS - 1, send, 0)
    own = pltpu.make_async_copy(
        grads.at[:, place, pl.ds(pl.multiple_of(head * ROWS, ROWS), ROWS)],
        landed.at[:, mine],
        own_sem,
    )
    own.start()
    own.wait()
    lax.fori_loop(0, PEERS - 1, wait, 0)

    for a, out in enumerate((dq_out, dk_out, dv_out)):
        wide[...] = landed[a].reshape(HEADS * ROWS, HD).astype(F32)
        for t in range(ROWS):
            out[t] = wide[pl.ds(t, HEADS, ROWS), :].astype(BF16)


def body(q, k, v, o, g):
    flat = [z.reshape(TOK * HL, HD) for z in (q, k, v, o, g)]
    vmem = pl.BlockSpec(memory_space=pltpu.VMEM)
    return pl.pallas_call(
        kernel,
        out_shape=[jax.ShapeDtypeStruct((ROWS, HEADS, HD), BF16)] * 3,
        in_specs=[vmem] * 5,
        out_specs=[vmem] * 3,
        scratch_shapes=[
            pltpu.VMEM((TOK * HL, HD), F32),
            pltpu.VMEM((4, HL, TOK, HD), BF16),
            pltpu.VMEM((HL, 8, TOK), F32),
            pltpu.VMEM((HL, TOK, HD), BF16),
            pltpu.VMEM((4, SPAN, TOK, HD), BF16),
            pltpu.VMEM((SPAN, 8, TOK), F32),
            pltpu.VMEM((3, SPAN, TOK, HD), BF16),
            pltpu.VMEM((3, HEADS, ROWS, HD), BF16),
            pltpu.SemaphoreType.DMA((4, SPAN)),
            pltpu.SemaphoreType.DMA((4, SPAN)),
            pltpu.SemaphoreType.DMA((SPAN,)),
            pltpu.SemaphoreType.DMA((SPAN,)),
            pltpu.SemaphoreType.DMA((PEERS,)),
            pltpu.SemaphoreType.DMA((PEERS,)),
            pltpu.SemaphoreType.DMA,
        ],
        compiler_params=pltpu.CompilerParams(
            collective_id=0, has_side_effects=True, vmem_limit_bytes=40 * 1024 * 1024
        ),
        name="grads",
    )(*flat)


def solution(mesh):
    placed = P("seq", "head", None)
    gathered = P(("seq", "head"), None, None)
    return jax.shard_map(
        body,
        mesh=mesh,
        in_specs=(placed,) * 5,
        out_specs=(gathered,) * 3,
        check_vma=False,
    )
```

time: 222 us -> 81.2 us (0.37)
  the two profiles are of different devices: /device:TPU:56 before, /device:TPU:1 now
where the time goes in v1:
time: 81.2 us; the launch traced here: 80.9 us
  Pallas kernels  73.4 us (90%)
  local copies, waits for them, and re-layouts  6.85 us (8%)
    pallas_call x1, Pallas kernels, body(): pl.pallas_call(kernel, out_shape=[jax.ShapeDtypeStruct((ROWS, HEADS, HD),...  73.4 us
    unnamed x13, local copies, waits for them, and re-layouts  6.85 us

profile of v1, /device:TPU:1, one launch (start us, length us, event | category | flops | bytes accessed | tf_op | source)
XLA Modules:
  0.0 80.9 jit_solution(7584649882925005702)
XLA Ops:
  0.6 0.0 copy-start
  0.6 0.9 %copy-done = bf16[256,4,128]{2,1,0:T(4,128)(2,1)S(1)} copy-done((bf16[256,4,128]{2,1,0:T(4,128)(2,1)S(1)}, bf16[256,4,128]{2,1,0:T(4,128)(2,1)}, u32[]{:S(2)}) %copy-start) | copy-done | bytes 262168
  1.6 0.0 copy-start.1
  1.6 0.9 %copy-done.1 = bf16[256,4,128]{2,1,0:T(4,128)(2,1)S(1)} copy-done((bf16[256,4,128]{2,1,0:T(4,128)(2,1)S(1)}, bf16[256,4,128]{2,1,0:T(4,128)(2,1)}, u32[]{:S(2)}) %copy-start.1) | copy-done | bytes 262168
  2.5 0.0 copy-start.2
  2.5 0.9 %copy-done.2 = bf16[256,4,128]{2,1,0:T(4,128)(2,1)S(1)} copy-done((bf16[256,4,128]{2,1,0:T(4,128)(2,1)S(1)}, bf16[256,4,128]{2,1,0:T(4,128)(2,1)}, u32[]{:S(2)}) %copy-start.2) | copy-done | bytes 262168
  3.5 0.0 copy-start.3
  3.5 0.9 %copy-done.3 = bf16[256,4,128]{2,1,0:T(4,128)(2,1)S(1)} copy-done((bf16[256,4,128]{2,1,0:T(4,128)(2,1)S(1)}, bf16[256,4,128]{2,1,0:T(4,128)(2,1)}, u32[]{:S(2)}) %copy-start.3) | copy-done | bytes 262168
  4.4 0.0 copy-start.4
  4.4 0.9 %copy-done.4 = bf16[256,4,128]{2,1,0:T(4,128)(2,1)S(1)} copy-done((bf16[256,4,128]{2,1,0:T(4,128)(2,1)S(1)}, bf16[256,4,128]{2,1,0:T(4,128)(2,1)}, u32[]{:S(2)}) %copy-start.4) | copy-done | bytes 262168
  5.4 73.4 %grads.1 = (bf16[32,32,128]{2,1,0:T(8,128)(2,1)S(1)}, bf16[32,32,128]{2,1,0:T(8,128)(2,1)S(1)}, bf16[32,32,128]{2,1,0:T(8,128)(2,1)S(1)}) custom-call(bf16[1024,128]{1,0:T(8,128)(2,1)S(1)} %bitcast.5, bf16[1024,128]{1,0:T(8,128)(2,1)S(1)} %bitcast.6, bf16[1024,128]{1,0:T(8,128)(2,1)S(1)} %bitcast.7, bf16[1024,128]{1,0:T(8,128)(2,1)S(1)} %bitcast.8, ...), custom_call_target="tpu_custom_call" | custom-call | tf_op jit(solution)/shard_map/grads/pallas_call | solution.py:210
  78.8 0.7 copy.11
  79.5 0.7 copy.12
  80.2 0.7 copy.13
Async XLA Ops:
  0.6 1.0 %copy-start = (bf16[256,4,128]{2,1,0:T(4,128)(2,1)S(1)}, bf16[256,4,128]{2,1,0:T(4,128)(2,1)}, u32[]{:S(2)}) copy-start(bf16[256,4,128]{2,1,0:T(4,128)(2,1)} %param.5) | copy-start | bytes 786436
  1.6 0.9 %copy-start.1 = (bf16[256,4,128]{2,1,0:T(4,128)(2,1)S(1)}, bf16[256,4,128]{2,1,0:T(4,128)(2,1)}, u32[]{:S(2)}) copy-start(bf16[256,4,128]{2,1,0:T(4,128)(2,1)} %param.6) | copy-start | bytes 786436
  2.5 0.9 %copy-start.2 = (bf16[256,4,128]{2,1,0:T(4,128)(2,1)S(1)}, bf16[256,4,128]{2,1,0:T(4,128)(2,1)}, u32[]{:S(2)}) copy-start(bf16[256,4,128]{2,1,0:T(4,128)(2,1)} %param.7) | copy-start | bytes 786436
  3.5 0.9 %copy-start.3 = (bf16[256,4,128]{2,1,0:T(4,128)(2,1)S(1)}, bf16[256,4,128]{2,1,0:T(4,128)(2,1)}, u32[]{:S(2)}) copy-start(bf16[256,4,128]{2,1,0:T(4,128)(2,1)} %param.8) | copy-start | bytes 786436
  4.4 0.9 %copy-start.4 = (bf16[256,4,128]{2,1,0:T(4,128)(2,1)S(1)}, bf16[256,4,128]{2,1,0:T(4,128)(2,1)}, u32[]{:S(2)}) copy-start(bf16[256,4,128]{2,1,0:T(4,128)(2,1)} %param.9) | copy-start | bytes 786436

commit v2 on v1

v2 whole, which is shorter than its diff:
```python
import functools

import jax
import jax.numpy as jnp
from jax import lax
from jax.experimental import pallas as pl
from jax.experimental.pallas import tpu as pltpu
from jax.sharding import PartitionSpec as P

MESH = pl.DeviceIdType.MESH
BF16 = jnp.bfloat16
F32 = jnp.float32
SPAN = 4
TOK = 256
HL = 4
HD = 128
HEADS = 32
PEERS = 32
ROWS = 32
SCALE = HD**-0.5
K, Q, G, V = range(4)

NT = (((1,), (1,)), ((), ()))


def dot(a, b):
    return jnp.dot(a, b, preferred_element_type=F32)


def dot_nt(a, b):
    return lax.dot_general(a, b, NT, preferred_element_type=F32)


def kernel(
    k_hbm, q_hbm, g_hbm, v_hbm, o_hbm,
    landed,
    stage, wide, send_in, send_corr, local_o, full, keys_t, corr, acc, grads,
    hbm_sem, in_send, in_recv, c_send, c_recv, out_send, out_recv, own_sem,
):
    seq = lax.axis_index("seq")
    head = lax.axis_index("head")
    base = (seq // SPAN) * SPAN
    place = seq % SPAN
    mine = head * HL + place

    def shifted(h, d):
        return ((h // 4 + d // 4) % 2) * 4 + (h % 4 + d % 4) % 4

    def back(h, d):
        return ((h // 4 + d // 4) % 2) * 4 + (h % 4 + 4 - d % 4) % 4

    loads = []
    for a, ref in enumerate((k_hbm, q_hbm, g_hbm, v_hbm, o_hbm)):
        loads.append(pltpu.make_async_copy(ref, stage.at[a], hbm_sem.at[a]))
        loads[-1].start()

    barrier = pltpu.get_barrier_semaphore()

    def greet(m, carry):
        to = (base + (place + SPAN - m % SPAN) % SPAN, back(head, m // SPAN))
        pl.semaphore_signal(barrier, inc=1, device_id=to, device_id_type=MESH)
        return carry

    lax.fori_loop(1, PEERS, greet, 0)

    def split_heads(a, store):
        loads[a].wait()
        wide[...] = stage[a].astype(F32)
        for h in range(HL):
            store(h, wide[pl.ds(h, TOK, HL), :].astype(BF16))

    def store_in(a):
        def store(h, rows):
            send_in[a, h] = rows

        return store

    def store_o(h, rows):
        local_o[h] = rows

    same_chip = place + 1 - 2 * (place % 2)
    others = (same_chip, (place + 2) % SPAN, (same_chip + 2) % SPAN)

    def in_copy(a, r):
        return pltpu.make_async_remote_copy(
            src_ref=send_in.at[a, others[r]],
            dst_ref=full.at[a, place],
            send_sem=in_send.at[a, r],
            recv_sem=in_recv.at[a, r],
            device_id=(base + others[r], head),
            device_id_type=MESH,
        )

    def corr_copy(r):
        return pltpu.make_async_remote_copy(
            src_ref=send_corr.at[others[r]],
            dst_ref=corr.at[place],
            send_sem=c_send.at[r],
            recv_sem=c_recv.at[r],
            device_id=(base + others[r], head),
            device_id_type=MESH,
        )

    split_heads(K, store_in(K))
    pl.semaphore_wait(barrier, PEERS - 1)
    for r in (1, 2, 0):
        in_copy(K, r).start()
    split_heads(V, store_in(V))

    @pl.when(place < 2)
    def _():
        for r in (1, 2, 0):
            in_copy(V, r).start()

    for a in (Q, G):
        split_heads(a, store_in(a))
        for r in (1, 2, 0):
            in_copy(a, r).start()

    @pl.when(place >= 2)
    def _():
        for r in (0, 1, 2):
            in_copy(V, r).start()

    split_heads(4, store_o)
    ones = jnp.ones((8, HD), BF16)
    for h in range(HL):
        prod = send_in[G, h].astype(F32) * local_o[h].astype(F32)
        high = prod.astype(BF16)
        low = (prod - high.astype(F32)).astype(BF16)
        send_corr[h] = dot_nt(ones, high) + dot_nt(ones, low)
    for r in (0, 1, 2):
        corr_copy(r).start()
    for a in range(4):
        full[a, place] = send_in[a, place]
    corr[place] = send_corr[place]

    def rows(i, first):
        q = full[Q, i]
        g = full[G, i]
        c = corr[i][0:1, :]
        row = lax.broadcasted_iota(jnp.int32, (TOK, TOK), 0)
        col = lax.broadcasted_iota(jnp.int32, (TOK, TOK), 1)
        scores = []
        for j in range(i + 1):
            s = dot_nt(full[K, j], q) * SCALE
            if i == j:
                s = jnp.where(row <= col, s, -jnp.inf)
            scores.append(s)
        top = jnp.max(scores[0], axis=0, keepdims=True)
        for s in scores[1:]:
            top = jnp.maximum(top, jnp.max(s, axis=0, keepdims=True))
        exps = [jnp.exp(s - top) for s in scores]
        total = jnp.sum(exps[0], axis=0, keepdims=True)
        for e in exps[1:]:
            total = total + jnp.sum(e, axis=0, keepdims=True)
        inv = 1.0 / total
        dq_t = jnp.zeros((HD, TOK), F32)
        for j in range(i + 1):
            w = exps[j] * inv
            dv = dot(w.astype(BF16), g)
            gw = dot_nt(full[V, j], g)
            ds = (w * (gw - c)).astype(BF16)
            dk = dot(ds, q)
            if j in first:
                acc[0, j] = acc[0, j] + dk
                acc[1, j] = acc[1, j] + dv
            else:
                acc[0, j] = dk
                acc[1, j] = dv
                first.add(j)
            dq_t = dq_t + dot(keys_t[j], ds)
        grads[0, i] = (dq_t * SCALE).T.astype(BF16)

    def finish(j):
        grads[1, j] = (acc[0, j] * SCALE).astype(BF16)
        grads[2, j] = acc[1, j].astype(BF16)

    def out_copy(a0, a1, p, d):
        to_head = shifted(head, d)
        m = d * SPAN + (p + SPAN - place) % SPAN
        return pltpu.make_async_remote_copy(
            src_ref=grads.at[a0:a1, p, pl.ds(pl.multiple_of(to_head * ROWS, ROWS), ROWS)],
            dst_ref=landed.at[a0:a1, mine],
            send_sem=out_send.at[m],
            recv_sem=out_recv.at[m],
            device_id=(base + p, to_head),
            device_id_type=MESH,
        )

    def own_copy(a0, a1):
        return pltpu.make_async_copy(
            grads.at[a0:a1, place, pl.ds(pl.multiple_of(head * ROWS, ROWS), ROWS)],
            landed.at[a0:a1, mine],
            own_sem,
        )

    def send(a0, a1, p0):
        def step(t, carry):
            d = (4 + t // 2) % 8
            p = p0 + t % 2
            me = jnp.logical_and(d == 0, p == place)

            @pl.when(me)
            def _():
                own_copy(a0, a1).start()

            @pl.when(jnp.logical_not(me))
            def _():
                out_copy(a0, a1, p, d).start()

            return carry

        lax.fori_loop(0, 16, step, 0)

    def turn(j):
        keys_t[j] = full[K, j].T

    for a in range(4):
        in_copy(a, 0).wait_recv()
    corr_copy(0).wait_recv()

    @pl.when(place < 2)
    def _():
        first = set()
        for i in (0, 1):
            turn(i)
            rows(i, first)
        send(0, 1, 0)
        for a in (K, Q, G, V):
            for r in (1, 2):
                in_copy(a, r).wait_recv()
        for r in (1, 2):
            corr_copy(r).wait_recv()
        turn(2)
        turn(3)
        rows(3, first)
        rows(2, first)
        for j in range(SPAN):
            finish(j)
        send(0, 3, 2)
        send(1, 3, 0)

    @pl.when(place >= 2)
    def _():
        first = set()
        turn(2)
        turn(3)
        for a in (K, V):
            for r in (1, 2):
                in_copy(a, r).wait_recv()
        turn(0)
        turn(1)
        rows(2, first)
        rows(3, first)
        finish(2)
        finish(3)
        send(0, 3, 2)
        for a in (Q, G):
            for r in (1, 2):
                in_copy(a, r).wait_recv()
        for r in (1, 2):
            corr_copy(r).wait_recv()
        rows(1, first)
        rows(0, first)
        finish(0)
        finish(1)
        send(0, 3, 0)

    for a in range(4):
        for r in range(3):
            in_copy(a, r).wait_send()
    for r in range(3):
        corr_copy(r).wait_send()
    own_copy(0, 3).wait()

    def wait(m, carry):
        out_copy(0, 3, (place + m) % SPAN, m // SPAN).wait()
        return carry

    lax.fori_loop(1, PEERS, wait, 0)


def arrange(landed_hbm, dq_out, dk_out, dv_out, landed, wide, done, in_sem, sem):
    loads = [
        pltpu.make_async_copy(landed_hbm.at[a], landed.at[a], in_sem.at[a]) for a in range(3)
    ]
    for load in loads:
        load.start()
    copies = []
    for a, out in enumerate((dq_out, dk_out, dv_out)):
        loads[a].wait()
        wide[a] = landed[a].reshape(HEADS * ROWS, HD).astype(F32)
        for t in range(ROWS):
            done[a, t] = wide[a, pl.ds(t, HEADS, ROWS), :].astype(BF16)
        copies.append(pltpu.make_async_copy(done.at[a], out, sem.at[a]))
        copies[-1].start()
    for copy in copies:
        copy.wait()


def body(q, k, v, o, g):
    flat = [z.reshape(TOK * HL, HD) for z in (k, q, g, v, o)]
    hbm = pl.BlockSpec(memory_space=pltpu.HBM)
    landed = pl.pallas_call(
        kernel,
        out_shape=jax.ShapeDtypeStruct((3, HEADS, ROWS, HD), BF16),
        in_specs=[hbm] * 5,
        out_specs=hbm,
        scratch_shapes=[
            pltpu.VMEM((5, TOK * HL, HD), BF16),
            pltpu.VMEM((TOK * HL, HD), F32),
            pltpu.VMEM((4, HL, TOK, HD), BF16),
            pltpu.VMEM((HL, 8, TOK), F32),
            pltpu.VMEM((HL, TOK, HD), BF16),
            pltpu.VMEM((4, SPAN, TOK, HD), BF16),
            pltpu.VMEM((SPAN, HD, TOK), BF16),
            pltpu.VMEM((SPAN, 8, TOK), F32),
            pltpu.VMEM((2, SPAN, TOK, HD), F32),
            pltpu.VMEM((3, SPAN, TOK, HD), BF16),
            pltpu.SemaphoreType.DMA((5,)),
            pltpu.SemaphoreType.DMA((4, 3)),
            pltpu.SemaphoreType.DMA((4, 3)),
            pltpu.SemaphoreType.DMA((3,)),
            pltpu.SemaphoreType.DMA((3,)),
            pltpu.SemaphoreType.DMA((PEERS,)),
            pltpu.SemaphoreType.DMA((PEERS,)),
            pltpu.SemaphoreType.DMA,
        ],
        compiler_params=pltpu.CompilerParams(
            collective_id=0, has_side_effects=True, vmem_limit_bytes=60 * 1024 * 1024
        ),
        name="grads",
    )(*flat)
    return pl.pallas_call(
        arrange,
        out_shape=[jax.ShapeDtypeStruct((ROWS, HEADS, HD), BF16)] * 3,
        in_specs=[hbm],
        out_specs=[hbm] * 3,
        scratch_shapes=[
            pltpu.VMEM((3, HEADS, ROWS, HD), BF16),
            pltpu.VMEM((3, HEADS * ROWS, HD), F32),
            pltpu.VMEM((3, ROWS, HEADS, HD), BF16),
            pltpu.SemaphoreType.DMA((3,)),
            pltpu.SemaphoreType.DMA((3,)),
        ],
        compiler_params=pltpu.CompilerParams(vmem_limit_bytes=60 * 1024 * 1024),
        name="arrange",
    )(landed)


def solution(mesh):
    placed = P("seq", "head", None)
    gathered = P(("seq", "head"), None, None)
    return jax.shard_map(
        body,
        mesh=mesh,
        in_specs=(placed,) * 5,
        out_specs=(gathered,) * 3,
        check_vma=False,
    )
```

time: 81.2 us -> 74.4 us (0.916)
  local copies, waits for them, and re-layouts: 6.85 us -> 0 us
    unnamed x13 -> x0, local copies, waits for them, and re-layouts: 6.85 us -> none
    pallas_call x1 -> x2, Pallas kernels: 73.4 us -> 73.6 us  [the longest x1 70.9 us: body(): pl.pallas_call(kernel, out_shape=jax.ShapeDtypeStruct((3, HEADS, ROWS, HD...]
where the time goes in v2:
time: 74.4 us; the launch traced here: 74.3 us
  Pallas kernels  73.6 us (99%)
    pallas_call x1, Pallas kernels, body(): pl.pallas_call(kernel, out_shape=jax.ShapeDtypeStruct((3, HEADS, ROWS, HD...  70.9 us
    pallas_call x1, Pallas kernels, body(): pl.pallas_call(arrange, out_shape=[jax.ShapeDtypeStruct((ROWS, HEADS, HD)...  2.7 us

profile of v2, /device:TPU:1, one launch (start us, length us, event | category | flops | bytes accessed | tf_op | source)
XLA Modules:
  0.0 74.3 jit_solution(14018998603578147054)
XLA Ops:
  0.6 70.9 %grads.1.landed_hbm = bf16[3,32,32,128]{3,2,1,0:T(8,128)(2,1)} custom-call(bf16[1024,128]{1,0:T(8,128)(2,1)} %bitcast.5, bf16[1024,128]{1,0:T(8,128)(2,1)} %bitcast.6, bf16[1024,128]{1,0:T(8,128)(2,1)} %bitcast.7, bf16[1024,128]{1,0:T(8,128)(2,1)} %bitcast.8, bf16[1024,128]{1,0:T(8,128)(2,1)} %bitcast.9), custom_call_target="tpu_custom_call" | custom-call | tf_op jit(solution)/shard_map/grads/pallas_call | solution.py:305
  71.6 2.7 %arrange.1 = (bf16[32,32,128]{2,1,0:T(8,128)(2,1)}, bf16[32,32,128]{2,1,0:T(8,128)(2,1)}, bf16[32,32,128]{2,1,0:T(8,128)(2,1)}) custom-call(bf16[3,32,32,128]{3,2,1,0:T(8,128)(2,1)} %grads.1.landed_hbm), custom_call_target="tpu_custom_call" | custom-call | tf_op jit(solution)/shard_map/arrange/pallas_call | solution.py:335

commit v3 on v2

--- a/solution.py
+++ b/solution.py
@@ -16,6 +16,7 @@
 HD = 128
 HEADS = 32
 PEERS = 32
+NEAR = 16
 ROWS = 32
 SCALE = HD**-0.5
 K, Q, G, V = range(4)
@@ -61,7 +62,8 @@
         pl.semaphore_signal(barrier, inc=1, device_id=to, device_id_type=MESH)
         return carry
 
-    lax.fori_loop(1, PEERS, greet, 0)
+    lax.fori_loop(1, NEAR, greet, 0)
+    upper = head >= 4
 
     def split_heads(a, store):
         loads[a].wait()
@@ -102,7 +104,15 @@
         )
 
     split_heads(K, store_in(K))
-    pl.semaphore_wait(barrier, PEERS - 1)
+    @pl.when(upper)
+    def _():
+        pl.semaphore_wait(barrier, PEERS - 1)
+
+    @pl.when(jnp.logical_not(upper))
+    def _():
+        pl.semaphore_wait(barrier, NEAR - 1)
+
+    lax.fori_loop(NEAR, PEERS, greet, 0)
     for r in (1, 2, 0):
         in_copy(K, r).start()
     split_heads(V, store_in(V))
@@ -195,9 +205,9 @@
             own_sem,
         )
 
-    def send(a0, a1, p0):
+    def send_half(a0, a1, p0, d0):
         def step(t, carry):
-            d = (4 + t // 2) % 8
+            d = d0 + t // 2
             p = p0 + t % 2
             me = jnp.logical_and(d == 0, p == place)
 
@@ -211,7 +221,14 @@
 
             return carry
 
-        lax.fori_loop(0, 16, step, 0)
+        lax.fori_loop(0, 8, step, 0)
+
+    def send(a0, a1, p0):
+        @pl.when(upper)
+        def _():
+            send_half(a0, a1, p0, 4)
+
+        send_half(a0, a1, p0, 0)
 
     def turn(j):
         keys_t[j] = full[K, j].T
@@ -266,6 +283,12 @@
         finish(0)
         finish(1)
         send(0, 3, 0)
+
+    @pl.when(jnp.logical_not(upper))
+    def _():
+        pl.semaphore_wait(barrier, PEERS - NEAR)
+        send_half(0, 3, 2, 4)
+        send_half(0, 3, 0, 4)
 
     for a in range(4):
         for r in range(3):

time: 74.4 us -> 78.6 us (1.056)
  Pallas kernels: 73.6 us -> 77.8 us
    pallas_call x1, Pallas kernels: 70.9 us -> 75.1 us  [body(): pl.pallas_call(kernel, out_shape=jax.ShapeDtypeStruct((3, HEADS, ROWS, HD...]
where the time goes in v3:
time: 78.6 us; the launch traced here: 78.5 us
  Pallas kernels  77.8 us (99%)
    pallas_call x1, Pallas kernels, body(): pl.pallas_call(kernel, out_shape=jax.ShapeDtypeStruct((3, HEADS, ROWS, HD...  75.1 us
    pallas_call x1, Pallas kernels, body(): pl.pallas_call(arrange, out_shape=[jax.ShapeDtypeStruct((ROWS, HEADS, HD)...  2.7 us

profile of v3, /device:TPU:1, one launch (start us, length us, event | category | flops | bytes accessed | tf_op | source)
XLA Modules:
  0.0 78.5 jit_solution(11591037463889579425)
XLA Ops:
  0.6 75.1 %grads.1.landed_hbm = bf16[3,32,32,128]{3,2,1,0:T(8,128)(2,1)} custom-call(bf16[1024,128]{1,0:T(8,128)(2,1)} %bitcast.5, bf16[1024,128]{1,0:T(8,128)(2,1)} %bitcast.6, bf16[1024,128]{1,0:T(8,128)(2,1)} %bitcast.7, bf16[1024,128]{1,0:T(8,128)(2,1)} %bitcast.8, bf16[1024,128]{1,0:T(8,128)(2,1)} %bitcast.9), custom_call_target="tpu_custom_call" | custom-call | tf_op jit(solution)/shard_map/grads/pallas_call | solution.py:328
  75.8 2.7 %arrange.1 = (bf16[32,32,128]{2,1,0:T(8,128)(2,1)}, bf16[32,32,128]{2,1,0:T(8,128)(2,1)}, bf16[32,32,128]{2,1,0:T(8,128)(2,1)}) custom-call(bf16[3,32,32,128]{3,2,1,0:T(8,128)(2,1)} %grads.1.landed_hbm), custom_call_target="tpu_custom_call" | custom-call | tf_op jit(solution)/shard_map/arrange/pallas_call | solution.py:358

commit v4 on v2

--- a/solution.py
+++ b/solution.py
@@ -16,6 +16,7 @@
 HD = 128
 HEADS = 32
 PEERS = 32
+NEAR = 16
 ROWS = 32
 SCALE = HD**-0.5
 K, Q, G, V = range(4)
@@ -61,7 +62,9 @@
         pl.semaphore_signal(barrier, inc=1, device_id=to, device_id_type=MESH)
         return carry
 
-    lax.fori_loop(1, PEERS, greet, 0)
+
+    lax.fori_loop(1, NEAR, greet, 0)
+    upper = head >= 4
 
     def split_heads(a, store):
         loads[a].wait()
@@ -102,6 +105,7 @@
         )
 
     split_heads(K, store_in(K))
+    lax.fori_loop(NEAR, PEERS, greet, 0)
     pl.semaphore_wait(barrier, PEERS - 1)
     for r in (1, 2, 0):
         in_copy(K, r).start()
@@ -195,23 +199,33 @@
             own_sem,
         )
 
-    def send(a0, a1, p0):
+    def send_half(parts, d0):
         def step(t, carry):
-            d = (4 + t // 2) % 8
-            p = p0 + t % 2
-            me = jnp.logical_and(d == 0, p == place)
-
-            @pl.when(me)
-            def _():
-                own_copy(a0, a1).start()
-
-            @pl.when(jnp.logical_not(me))
-            def _():
-                out_copy(a0, a1, p, d).start()
+            d = d0 + t // 2
+            for a0, a1, p0 in parts:
+                p = p0 + t % 2
+                me = jnp.logical_and(d == 0, p == place)
+
+                @pl.when(me)
+                def _():
+                    own_copy(a0, a1).start()
+
+                @pl.when(jnp.logical_not(me))
+                def _():
+                    out_copy(a0, a1, p, d).start()
 
             return carry
 
-        lax.fori_loop(0, 16, step, 0)
+        lax.fori_loop(0, 8, step, 0)
+
+    def send(*parts):
+        send_half(parts, 4)
+        send_half(parts, 0)
+
+    def answer():
+        @pl.when(upper)
+        def _():
+            lax.fori_loop(NEAR, PEERS, greet, 0)
 
     def turn(j):
         keys_t[j] = full[K, j].T
@@ -226,7 +240,7 @@
         for i in (0, 1):
             turn(i)
             rows(i, first)
-        send(0, 1, 0)
+        send((0, 1, 0))
         for a in (K, Q, G, V):
             for r in (1, 2):
                 in_copy(a, r).wait_recv()
@@ -238,8 +252,7 @@
         rows(2, first)
         for j in range(SPAN):
             finish(j)
-        send(0, 3, 2)
-        send(1, 3, 0)
+        send((0, 3, 2), (1, 3, 0))
 
     @pl.when(place >= 2)
     def _():
@@ -255,7 +268,7 @@
         rows(3, first)
         finish(2)
         finish(3)
-        send(0, 3, 2)
+        send((0, 3, 2))
         for a in (Q, G):
             for r in (1, 2):
                 in_copy(a, r).wait_recv()
@@ -265,7 +278,7 @@
         rows(0, first)
         finish(0)
         finish(1)
-        send(0, 3, 0)
+        send((0, 3, 0))
 
     for a in range(4):
         for r in range(3):

time: 74.4 us -> 70.6 us (0.949)
  Pallas kernels: 73.6 us -> 69.2 us
    pallas_call x1, Pallas kernels: 70.9 us -> 66.5 us  [body(): pl.pallas_call(kernel, out_shape=jax.ShapeDtypeStruct((3, HEADS, ROWS, HD...]
where the time goes in v4:
time: 70.6 us; the launch traced here: 69.8 us
  Pallas kernels  69.2 us (98%)
    pallas_call x1, Pallas kernels, body(): pl.pallas_call(kernel, out_shape=jax.ShapeDtypeStruct((3, HEADS, ROWS, HD...  66.5 us
    pallas_call x1, Pallas kernels, body(): pl.pallas_call(arrange, out_shape=[jax.ShapeDtypeStruct((ROWS, HEADS, HD)...  2.7 us

profile of v4, /device:TPU:1, one launch (start us, length us, event | category | flops | bytes accessed | tf_op | source)
XLA Modules:
  0.0 69.8 jit_solution(8914601724463126465)
XLA Ops:
  0.6 66.5 %grads.1.landed_hbm = bf16[3,32,32,128]{3,2,1,0:T(8,128)(2,1)} custom-call(bf16[1024,128]{1,0:T(8,128)(2,1)} %bitcast.5, bf16[1024,128]{1,0:T(8,128)(2,1)} %bitcast.6, bf16[1024,128]{1,0:T(8,128)(2,1)} %bitcast.7, bf16[1024,128]{1,0:T(8,128)(2,1)} %bitcast.8, bf16[1024,128]{1,0:T(8,128)(2,1)} %bitcast.9), custom_call_target="tpu_custom_call" | custom-call | tf_op jit(solution)/shard_map/grads/pallas_call | solution.py:318
  67.1 2.7 %arrange.1 = (bf16[32,32,128]{2,1,0:T(8,128)(2,1)}, bf16[32,32,128]{2,1,0:T(8,128)(2,1)}, bf16[32,32,128]{2,1,0:T(8,128)(2,1)}) custom-call(bf16[3,32,32,128]{3,2,1,0:T(8,128)(2,1)} %grads.1.landed_hbm), custom_call_target="tpu_custom_call" | custom-call | tf_op jit(solution)/shard_map/arrange/pallas_call | solution.py:348

commit v5 on v4

--- a/solution.py
+++ b/solution.py
@@ -35,7 +35,7 @@
 def kernel(
     k_hbm, q_hbm, g_hbm, v_hbm, o_hbm,
     landed,
-    stage, wide, send_in, send_corr, local_o, full, keys_t, corr, acc, grads,
+    stage, wide, send_in, send_corr, local_o, full, keys_t, corr, acc, held_w, held_q, grads,
     hbm_sem, in_send, in_recv, c_send, c_recv, out_send, out_recv, own_sem,
 ):
     seq = lax.axis_index("seq")
@@ -61,7 +61,6 @@
         to = (base + (place + SPAN - m % SPAN) % SPAN, back(head, m // SPAN))
         pl.semaphore_signal(barrier, inc=1, device_id=to, device_id_type=MESH)
         return carry
-
 
     lax.fori_loop(1, NEAR, greet, 0)
     upper = head >= 4
@@ -105,8 +104,14 @@
         )
 
     split_heads(K, store_in(K))
-    lax.fori_loop(NEAR, PEERS, greet, 0)
-    pl.semaphore_wait(barrier, PEERS - 1)
+    @pl.when(upper)
+    def _():
+        pl.semaphore_wait(barrier, PEERS - 1)
+
+    @pl.when(jnp.logical_not(upper))
+    def _():
+        pl.semaphore_wait(barrier, NEAR - 1)
+        lax.fori_loop(NEAR, PEERS, greet, 0)
     for r in (1, 2, 0):
         in_copy(K, r).start()
     split_heads(V, store_in(V))
@@ -139,10 +144,23 @@
         full[a, place] = send_in[a, place]
     corr[place] = send_corr[place]
 
-    def rows(i, first):
+    def add(a, j, term, first):
+        if (a, j) in first:
+            term = acc[a, j] + term
+        acc[a, j] = term
+        first.add((a, j))
+
+    def pair(i, j, w, first):
         q = full[Q, i]
         g = full[G, i]
-        c = corr[i][0:1, :]
+        gw = dot_nt(full[V, j], g)
+        ds = (w * (gw - corr[i][0:1, :])).astype(BF16)
+        add(0, j, dot(ds, q), first)
+        return dot(keys_t[j], ds)
+
+    def rows(i, first, end=SPAN):
+        q = full[Q, i]
+        g = full[G, i]
         row = lax.broadcasted_iota(jnp.int32, (TOK, TOK), 0)
         col = lax.broadcasted_iota(jnp.int32, (TOK, TOK), 1)
         scores = []
@@ -162,18 +180,20 @@
         dq_t = jnp.zeros((HD, TOK), F32)
         for j in range(i + 1):
             w = exps[j] * inv
-            dv = dot(w.astype(BF16), g)
-            gw = dot_nt(full[V, j], g)
-            ds = (w * (gw - c)).astype(BF16)
-            dk = dot(ds, q)
-            if j in first:
-                acc[0, j] = acc[0, j] + dk
-                acc[1, j] = acc[1, j] + dv
+            add(1, j, dot(w.astype(BF16), g), first)
+            if j < end:
+                dq_t = dq_t + pair(i, j, w, first)
             else:
-                acc[0, j] = dk
-                acc[1, j] = dv
-                first.add(j)
-            dq_t = dq_t + dot(keys_t[j], ds)
+                held_w[i + j - 4] = w
+        if i < end:
+            grads[0, i] = (dq_t * SCALE).T.astype(BF16)
+        else:
+            held_q[i - 2] = dq_t
+
+    def rest(i, first):
+        dq_t = held_q[i - 2]
+        for j in range(2, i + 1):
+            dq_t = dq_t + pair(i, j, held_w[i + j - 4], first)
         grads[0, i] = (dq_t * SCALE).T.astype(BF16)
 
     def finish(j):
@@ -219,7 +239,10 @@
         lax.fori_loop(0, 8, step, 0)
 
     def send(*parts):
-        send_half(parts, 4)
+        @pl.when(upper)
+        def _():
+            send_half(parts, 4)
+
         send_half(parts, 0)
 
     def answer():
@@ -237,22 +260,30 @@
     @pl.when(place < 2)
     def _():
         first = set()
+        answer()
         for i in (0, 1):
             turn(i)
             rows(i, first)
         send((0, 1, 0))
-        for a in (K, Q, G, V):
+        for a in (K, Q, G):
             for r in (1, 2):
                 in_copy(a, r).wait_recv()
         for r in (1, 2):
             corr_copy(r).wait_recv()
         turn(2)
         turn(3)
-        rows(3, first)
-        rows(2, first)
-        for j in range(SPAN):
-            finish(j)
-        send((0, 3, 2), (1, 3, 0))
+        rows(2, first, 2)
+        rows(3, first, 2)
+        finish(0)
+        finish(1)
+        send((1, 3, 0))
+        for r in (1, 2):
+            in_copy(V, r).wait_recv()
+        rest(2, first)
+        rest(3, first)
+        finish(2)
+        finish(3)
+        send((0, 3, 2))
 
     @pl.when(place >= 2)
     def _():
@@ -262,6 +293,7 @@
         for a in (K, V):
             for r in (1, 2):
                 in_copy(a, r).wait_recv()
+        answer()
         turn(0)
         turn(1)
         rows(2, first)
@@ -279,6 +311,11 @@
         finish(0)
         finish(1)
         send((0, 3, 0))
+
+    @pl.when(jnp.logical_not(upper))
+    def _():
+        pl.semaphore_wait(barrier, PEERS - NEAR)
+        send_half(((0, 3, 2), (0, 3, 0)), 4)
 
     for a in range(4):
         for r in range(3):
@@ -330,6 +367,8 @@
             pltpu.VMEM((SPAN, HD, TOK), BF16),
             pltpu.VMEM((SPAN, 8, TOK), F32),
             pltpu.VMEM((2, SPAN, TOK, HD), F32),
+            pltpu.VMEM((3, TOK, TOK), F32),
+            pltpu.VMEM((2, HD, TOK), F32),
             pltpu.VMEM((3, SPAN, TOK, HD), BF16),
             pltpu.SemaphoreType.DMA((5,)),
             pltpu.SemaphoreType.DMA((4, 3)),

time: 70.6 us -> 68.5 us (0.970)
  the two profiles are of different devices: /device:TPU:1 before, /device:TPU:219 now
where the time goes in v5:
time: 68.5 us; the launch traced here: 68.3 us
  Pallas kernels  67.7 us (99%)
    pallas_call x1, Pallas kernels, body(): pl.pallas_call(kernel, out_shape=jax.ShapeDtypeStruct((3, HEADS, ROWS, HD...  65 us
    pallas_call x1, Pallas kernels, body(): pl.pallas_call(arrange, out_shape=[jax.ShapeDtypeStruct((ROWS, HEADS, HD)...  2.7 us

profile of v5, /device:TPU:219, one launch (start us, length us, event | category | flops | bytes accessed | tf_op | source)
XLA Modules:
  0.0 68.3 jit_solution(10677926236257415247)
XLA Ops:
  0.6 65.0 %grads.1.landed_hbm = bf16[3,32,32,128]{3,2,1,0:T(8,128)(2,1)} custom-call(bf16[1024,128]{1,0:T(8,128)(2,1)} %bitcast.5, bf16[1024,128]{1,0:T(8,128)(2,1)} %bitcast.6, bf16[1024,128]{1,0:T(8,128)(2,1)} %bitcast.7, bf16[1024,128]{1,0:T(8,128)(2,1)} %bitcast.8, bf16[1024,128]{1,0:T(8,128)(2,1)} %bitcast.9), custom_call_target="tpu_custom_call" | custom-call | tf_op jit(solution)/shard_map/grads/pallas_call | solution.py:355
  65.6 2.7 %arrange.1 = (bf16[32,32,128]{2,1,0:T(8,128)(2,1)}, bf16[32,32,128]{2,1,0:T(8,128)(2,1)}, bf16[32,32,128]{2,1,0:T(8,128)(2,1)}) custom-call(bf16[3,32,32,128]{3,2,1,0:T(8,128)(2,1)} %grads.1.landed_hbm), custom_call_target="tpu_custom_call" | custom-call | tf_op jit(solution)/shard_map/arrange/pallas_call | solution.py:387

commit v6 on v5

--- a/solution.py
+++ b/solution.py
@@ -12,6 +12,7 @@
 F32 = jnp.float32
 SPAN = 4
 TOK = 256
+CHIP = 2 * TOK
 HL = 4
 HD = 128
 HEADS = 32
@@ -19,6 +20,8 @@
 NEAR = 16
 ROWS = 32
 SCALE = HD**-0.5
+LOG2E = 1.4426950408889634
+PIECE = 16
 K, Q, G, V = range(4)
 
 NT = (((1,), (1,)), ((), ()))
@@ -72,10 +75,10 @@
             store(h, wide[pl.ds(h, TOK, HL), :].astype(BF16))
 
     def store_in(a):
-        def store(h, rows):
+        def put(h, rows):
             send_in[a, h] = rows
 
-        return store
+        return put
 
     def store_o(h, rows):
         local_o[h] = rows
@@ -150,62 +153,71 @@
         acc[a, j] = term
         first.add((a, j))
 
+    def part(a, i):
+        return full[a, 2 * i : 2 * i + 2].reshape(CHIP, HD)
+
     def pair(i, j, w, first):
-        q = full[Q, i]
-        g = full[G, i]
-        gw = dot_nt(full[V, j], g)
-        ds = (w * (gw - corr[i][0:1, :])).astype(BF16)
-        add(0, j, dot(ds, q), first)
+        gw = dot_nt(part(V, j), part(G, i))
+        c = jnp.concatenate([corr[2 * i, 0:1], corr[2 * i + 1, 0:1]], axis=1)
+        ds = (w * (gw - c)).astype(BF16)
+        add(0, j, dot(ds, part(Q, i)), first)
         return dot(keys_t[j], ds)
 
-    def rows(i, first, end=SPAN):
-        q = full[Q, i]
-        g = full[G, i]
-        row = lax.broadcasted_iota(jnp.int32, (TOK, TOK), 0)
-        col = lax.broadcasted_iota(jnp.int32, (TOK, TOK), 1)
+    def store(a, i, term):
+        term = term.astype(BF16).reshape(2, TOK // ROWS, ROWS, HD)
+        grads[2 * i : 2 * i + 2, :, a] = term
+
+    def store_dq(i, dq_t):
+        store(0, i, (dq_t * SCALE).T)
+
+    def rows(i, first, hold=None):
+        q = part(Q, i)
+        g = part(G, i)
+        row = lax.broadcasted_iota(jnp.int32, (CHIP, CHIP), 0)
+        col = lax.broadcasted_iota(jnp.int32, (CHIP, CHIP), 1)
         scores = []
         for j in range(i + 1):
-            s = dot_nt(full[K, j], q) * SCALE
+            s = dot_nt(part(K, j), q) * (SCALE * LOG2E)
             if i == j:
                 s = jnp.where(row <= col, s, -jnp.inf)
             scores.append(s)
         top = jnp.max(scores[0], axis=0, keepdims=True)
         for s in scores[1:]:
             top = jnp.maximum(top, jnp.max(s, axis=0, keepdims=True))
-        exps = [jnp.exp(s - top) for s in scores]
+        exps = [jnp.exp2(s - top) for s in scores]
         total = jnp.sum(exps[0], axis=0, keepdims=True)
         for e in exps[1:]:
             total = total + jnp.sum(e, axis=0, keepdims=True)
         inv = 1.0 / total
-        dq_t = jnp.zeros((HD, TOK), F32)
+        dq_t = jnp.zeros((HD, CHIP), F32)
         for j in range(i + 1):
             w = exps[j] * inv
-            add(1, j, dot(w.astype(BF16), g), first)
-            if j < end:
+            if j == hold:
+                held_w[...] = w
+            else:
                 dq_t = dq_t + pair(i, j, w, first)
-            else:
-                held_w[i + j - 4] = w
-        if i < end:
-            grads[0, i] = (dq_t * SCALE).T.astype(BF16)
+            if j != hold or j == i:
+                add(1, j, dot(w.astype(BF16), g), first)
+        if hold is None:
+            store_dq(i, dq_t)
         else:
-            held_q[i - 2] = dq_t
-
-    def rest(i, first):
-        dq_t = held_q[i - 2]
-        for j in range(2, i + 1):
-            dq_t = dq_t + pair(i, j, held_w[i + j - 4], first)
-        grads[0, i] = (dq_t * SCALE).T.astype(BF16)
+            held_q[...] = dq_t
+
+    def rest(hold, first):
+        w = held_w[...]
+        store_dq(1, held_q[...] + pair(1, hold, w, first))
+        return w
 
     def finish(j):
-        grads[1, j] = (acc[0, j] * SCALE).astype(BF16)
-        grads[2, j] = acc[1, j].astype(BF16)
+        store(1, j, acc[0, j] * SCALE)
+        store(2, j, acc[1, j])
 
     def out_copy(a0, a1, p, d):
         to_head = shifted(head, d)
         m = d * SPAN + (p + SPAN - place) % SPAN
         return pltpu.make_async_remote_copy(
-            src_ref=grads.at[a0:a1, p, pl.ds(pl.multiple_of(to_head * ROWS, ROWS), ROWS)],
-            dst_ref=landed.at[a0:a1, mine],
+            src_ref=grads.at[p, to_head, a0:a1],
+            dst_ref=landed.at[mine, a0:a1],
             send_sem=out_send.at[m],
             recv_sem=out_recv.at[m],
             device_id=(base + p, to_head),
@@ -214,8 +226,8 @@
 
     def own_copy(a0, a1):
         return pltpu.make_async_copy(
-            grads.at[a0:a1, place, pl.ds(pl.multiple_of(head * ROWS, ROWS), ROWS)],
-            landed.at[a0:a1, mine],
+            grads.at[place, head, a0:a1],
+            landed.at[mine, a0:a1],
             own_sem,
         )
 
@@ -251,7 +263,7 @@
             lax.fori_loop(NEAR, PEERS, greet, 0)
 
     def turn(j):
-        keys_t[j] = full[K, j].T
+        keys_t[j] = part(K, j).T
 
     for a in range(4):
         in_copy(a, 0).wait_recv()
@@ -261,55 +273,47 @@
     def _():
         first = set()
         answer()
-        for i in (0, 1):
-            turn(i)
-            rows(i, first)
+        turn(0)
+        rows(0, first)
         send((0, 1, 0))
         for a in (K, Q, G):
             for r in (1, 2):
                 in_copy(a, r).wait_recv()
         for r in (1, 2):
             corr_copy(r).wait_recv()
-        turn(2)
-        turn(3)
-        rows(2, first, 2)
-        rows(3, first, 2)
+        turn(1)
+        rows(1, first, hold=1)
         finish(0)
-        finish(1)
         send((1, 3, 0))
         for r in (1, 2):
             in_copy(V, r).wait_recv()
-        rest(2, first)
-        rest(3, first)
-        finish(2)
-        finish(3)
+        rest(1, first)
+        finish(1)
         send((0, 3, 2))
 
     @pl.when(place >= 2)
     def _():
         first = set()
-        turn(2)
-        turn(3)
-        for a in (K, V):
-            for r in (1, 2):
-                in_copy(a, r).wait_recv()
+        turn(1)
+        for r in (1, 2):
+            in_copy(K, r).wait_recv()
+        turn(0)
+        rows(1, first, hold=0)
         answer()
-        turn(0)
-        turn(1)
-        rows(2, first)
-        rows(3, first)
-        finish(2)
-        finish(3)
-        send((0, 3, 2))
+        finish(1)
+        send((1, 3, 2))
+        for r in (1, 2):
+            in_copy(V, r).wait_recv()
+        w = rest(0, first)
+        send((0, 1, 2))
+        add(1, 0, dot(w.astype(BF16), part(G, 1)), first)
         for a in (Q, G):
             for r in (1, 2):
                 in_copy(a, r).wait_recv()
         for r in (1, 2):
             corr_copy(r).wait_recv()
-        rows(1, first)
         rows(0, first)
         finish(0)
-        finish(1)
         send((0, 3, 0))
 
     @pl.when(jnp.logical_not(upper))
@@ -331,22 +335,30 @@
     lax.fori_loop(1, PEERS, wait, 0)
 
 
-def arrange(landed_hbm, dq_out, dk_out, dv_out, landed, wide, done, in_sem, sem):
-    loads = [
-        pltpu.make_async_copy(landed_hbm.at[a], landed.at[a], in_sem.at[a]) for a in range(3)
-    ]
-    for load in loads:
-        load.start()
-    copies = []
-    for a, out in enumerate((dq_out, dk_out, dv_out)):
-        loads[a].wait()
-        wide[a] = landed[a].reshape(HEADS * ROWS, HD).astype(F32)
-        for t in range(ROWS):
-            done[a, t] = wide[a, pl.ds(t, HEADS, ROWS), :].astype(BF16)
-        copies.append(pltpu.make_async_copy(done.at[a], out, sem.at[a]))
-        copies[-1].start()
-    for copy in copies:
-        copy.wait()
+def arrange(landed_hbm, dq_out, dk_out, dv_out, landed, wide, done, in_sem, out_sem):
+    pieces = [(a, h) for a in range(3) for h in range(ROWS // PIECE)]
+
+    def load(a, h):
+        return pltpu.make_async_copy(
+            landed_hbm.at[:, a, pl.ds(h * PIECE, PIECE)], landed.at[a, h], in_sem.at[a, h]
+        )
+
+    def store(a, h):
+        out = (dq_out, dk_out, dv_out)[a]
+        return pltpu.make_async_copy(
+            done.at[a, h], out.at[pl.ds(h * PIECE, PIECE)], out_sem.at[a, h]
+        )
+
+    for a, h in pieces:
+        load(a, h).start()
+    for a, h in pieces:
+        load(a, h).wait()
+        wide[a, h] = landed[a, h].reshape(HEADS * PIECE, HD).astype(F32)
+        for t in range(PIECE):
+            done[a, h, t] = wide[a, h, pl.ds(t, HEADS, PIECE), :].astype(BF16)
+        store(a, h).start()
+    for a, h in pieces:
+        store(a, h).wait()
 
 
 def body(q, k, v, o, g):
@@ -354,7 +366,7 @@
     hbm = pl.BlockSpec(memory_space=pltpu.HBM)
     landed = pl.pallas_call(
         kernel,
-        out_shape=jax.ShapeDtypeStruct((3, HEADS, ROWS, HD), BF16),
+        out_shape=jax.ShapeDtypeStruct((HEADS, 3, ROWS, HD), BF16),
         in_specs=[hbm] * 5,
         out_specs=hbm,
         scratch_shapes=[
@@ -364,12 +376,12 @@
             pltpu.VMEM((HL, 8, TOK), F32),
             pltpu.VMEM((HL, TOK, HD), BF16),
             pltpu.VMEM((4, SPAN, TOK, HD), BF16),
-            pltpu.VMEM((SPAN, HD, TOK), BF16),
+            pltpu.VMEM((2, HD, CHIP), BF16),
             pltpu.VMEM((SPAN, 8, TOK), F32),
-            pltpu.VMEM((2, SPAN, TOK, HD), F32),
-            pltpu.VMEM((3, TOK, TOK), F32),
-            pltpu.VMEM((2, HD, TOK), F32),
-            pltpu.VMEM((3, SPAN, TOK, HD), BF16),
+            pltpu.VMEM((2, 2, CHIP, HD), F32),
+            pltpu.VMEM((CHIP, CHIP), F32),
+            pltpu.VMEM((HD, CHIP), F32),
+            pltpu.VMEM((SPAN, TOK // ROWS, 3, ROWS, HD), BF16),
             pltpu.SemaphoreType.DMA((5,)),
             pltpu.SemaphoreType.DMA((4, 3)),
             pltpu.SemaphoreType.DMA((4, 3)),
@@ -390,11 +402,11 @@
         in_specs=[hbm],
         out_specs=[hbm] * 3,
         scratch_shapes=[
-            pltpu.VMEM((3, HEADS, ROWS, HD), BF16),
-            pltpu.VMEM((3, HEADS * ROWS, HD), F32),
-            pltpu.VMEM((3, ROWS, HEADS, HD), BF16),
-            pltpu.SemaphoreType.DMA((3,)),
-            pltpu.SemaphoreType.DMA((3,)),
+            pltpu.VMEM((3, ROWS // PIECE, HEADS, PIECE, HD), BF16),
+            pltpu.VMEM((3, ROWS // PIECE, HEADS * PIECE, HD), F32),
+            pltpu.VMEM((3, ROWS // PIECE, PIECE, HEADS, HD), BF16),
+            pltpu.SemaphoreType.DMA((3, ROWS // PIECE)),
+            pltpu.SemaphoreType.DMA((3, ROWS // PIECE)),
         ],
         compiler_params=pltpu.CompilerParams(vmem_limit_bytes=60 * 1024 * 1024),
         name="arrange",

time: 68.5 us -> 68 us (level)
  no operation moved by 1% of the time
where the time goes in v6:
time: 68 us; the launch traced here: 67.9 us
  Pallas kernels  67.2 us (99%)
    pallas_call x1, Pallas kernels, body(): pl.pallas_call(kernel, out_shape=jax.ShapeDtypeStruct((HEADS, 3, ROWS, HD...  65 us
    pallas_call x1, Pallas kernels, body(): pl.pallas_call(arrange, out_shape=[jax.ShapeDtypeStruct((ROWS, HEADS, HD)...  2.25 us

profile of v6, /device:TPU:219, one launch (start us, length us, event | category | flops | bytes accessed | tf_op | source)
XLA Modules:
  0.0 67.9 jit_solution(9222191762295722220)
XLA Ops:
  0.6 65.0 %grads.1.landed_hbm = bf16[32,3,32,128]{3,2,1,0:T(8,128)(2,1)} custom-call(bf16[1024,128]{1,0:T(8,128)(2,1)} %bitcast.5, bf16[1024,128]{1,0:T(8,128)(2,1)} %bitcast.6, bf16[1024,128]{1,0:T(8,128)(2,1)} %bitcast.7, bf16[1024,128]{1,0:T(8,128)(2,1)} %bitcast.8, bf16[1024,128]{1,0:T(8,128)(2,1)} %bitcast.9), custom_call_target="tpu_custom_call" | custom-call | tf_op jit(solution)/shard_map/grads/pallas_call | solution.py:367
  65.6 2.2 %arrange.1 = (bf16[32,32,128]{2,1,0:T(8,128)(2,1)}, bf16[32,32,128]{2,1,0:T(8,128)(2,1)}, bf16[32,32,128]{2,1,0:T(8,128)(2,1)}) custom-call(bf16[32,3,32,128]{3,2,1,0:T(8,128)(2,1)} %grads.1.landed_hbm), custom_call_target="tpu_custom_call" | custom-call | tf_op jit(solution)/shard_map/arrange/pallas_call | solution.py:399

commit v7 on v6

--- a/solution.py
+++ b/solution.py
@@ -67,6 +67,7 @@
 
     lax.fori_loop(1, NEAR, greet, 0)
     upper = head >= 4
+    prompt = (seq // SPAN) % 4 == 3
 
     def split_heads(a, store):
         loads[a].wait()
@@ -110,6 +111,10 @@
     @pl.when(upper)
     def _():
         pl.semaphore_wait(barrier, PEERS - 1)
+
+    @pl.when(jnp.logical_and(upper, prompt))
+    def _():
+        lax.fori_loop(NEAR, PEERS, greet, 0)
 
     @pl.when(jnp.logical_not(upper))
     def _():
@@ -258,7 +263,7 @@
         send_half(parts, 0)
 
     def answer():
-        @pl.when(upper)
+        @pl.when(jnp.logical_and(upper, jnp.logical_not(prompt)))
         def _():
             lax.fori_loop(NEAR, PEERS, greet, 0)
 

time: 68 us -> 68.2 us (level)
  the two profiles are of different devices: /device:TPU:219 before, /device:TPU:195 now
where the time goes in v7:
time: 68.2 us; the launch traced here: 68 us
  Pallas kernels  67.4 us (99%)
    pallas_call x1, Pallas kernels, body(): pl.pallas_call(kernel, out_shape=jax.ShapeDtypeStruct((HEADS, 3, ROWS, HD...  65.2 us
    pallas_call x1, Pallas kernels, body(): pl.pallas_call(arrange, out_shape=[jax.ShapeDtypeStruct((ROWS, HEADS, HD)...  2.25 us

profile of v7, /device:TPU:195, one launch (start us, length us, event | category | flops | bytes accessed | tf_op | source)
XLA Modules:
  0.0 68.0 jit_solution(4929422813999351887)
XLA Ops:
  0.6 65.2 %grads.1.landed_hbm = bf16[32,3,32,128]{3,2,1,0:T(8,128)(2,1)} custom-call(bf16[1024,128]{1,0:T(8,128)(2,1)} %bitcast.5, bf16[1024,128]{1,0:T(8,128)(2,1)} %bitcast.6, bf16[1024,128]{1,0:T(8,128)(2,1)} %bitcast.7, bf16[1024,128]{1,0:T(8,128)(2,1)} %bitcast.8, bf16[1024,128]{1,0:T(8,128)(2,1)} %bitcast.9), custom_call_target="tpu_custom_call" | custom-call | tf_op jit(solution)/shard_map/grads/pallas_call | solution.py:372
  65.8 2.2 %arrange.1 = (bf16[32,32,128]{2,1,0:T(8,128)(2,1)}, bf16[32,32,128]{2,1,0:T(8,128)(2,1)}, bf16[32,32,128]{2,1,0:T(8,128)(2,1)}) custom-call(bf16[32,3,32,128]{3,2,1,0:T(8,128)(2,1)} %grads.1.landed_hbm), custom_call_target="tpu_custom_call" | custom-call | tf_op jit(solution)/shard_map/arrange/pallas_call | solution.py:404
